TPU v7x, 32 devices: a whole 2x2x4 slice. The times are simulated.
32 devices in a mesh: ctx: 8 (over z, x), dp: 4 (over y, core).
Axes of the slice: x: 2, y: 2, z: 4, core: 2. Of those that a mesh axis runs over, the one named last changes fastest.
Arguments:
- query: bfloat16 [4, 4096, 1024], P('dp', 'ctx'), may hold values from -6 to 6
- key: bfloat16 [4, 4096, 1024], P('dp', 'ctx'), may hold values from -6 to 6
- value: bfloat16 [4, 4096, 1024], P('dp', 'ctx'), may hold values from -12 to 12
- log_decay: float32 [4, 8, 4096], P('dp', None, 'ctx'), may hold values from -2 to 0
- grad_out: bfloat16 [4, 4096, 1024], P('dp', 'ctx'), may hold values from -32 to 32
- query_map: bfloat16 [8, 128, 128], replicated, may hold values from -0.5 to 0.5
- key_map: bfloat16 [8, 128, 128], replicated, may hold values from -0.5 to 0.5
Outputs:
- output: bfloat16 [4, 4096, 1024], P('dp', 'ctx')
- grad_query: bfloat16 [4, 4096, 1024], P('dp', 'ctx')
- grad_key: bfloat16 [4, 4096, 1024], P('dp', 'ctx')
- grad_value: bfloat16 [4, 4096, 1024], P('dp', 'ctx')
- query_map_grad: float32 [8, 128, 128], replicated
- key_map_grad: float32 [8, 128, 128], replicated
All inputs are finite; a program needn't handle non-finite values.
Results may differ from a plain program's by a relative error of at most 0.0073.
Values sent between devices are 32-bit elements; how exact they have to be, the bound alone decides.
A program may use at most 128 MiB of HBM per device.

v0:
```python
import math

import jax
import jax.numpy as jnp
from jax import lax
from jax.sharding import PartitionSpec as P

BLOCK = 256


def prefix(value, axis, combine, identity, reverse):
    count, mine = (lax.axis_size(axis), lax.axis_index(axis))
    everything = jax.tree.map(lambda part: lax.all_gather(part, axis), value)
    start = jax.tree.map(
        lambda part, zero: jnp.broadcast_to(jnp.asarray(zero, part.dtype), part.shape),
        value,
        identity,
    )

    def step(k, before):
        at = count - 1 - k if reverse else k
        reached = at > mine if reverse else at < mine
        new = combine(before, jax.tree.map(lambda part: part[at], everything))
        return jax.tree.map(lambda a, b: jnp.where(reached, a, b), new, before)

    return lax.fori_loop(0, count, step, start)


def combine(earlier, latter):
    return (earlier[0] * latter[0], latter[0][:, None, None] * earlier[1] + latter[1])


def silu_slope(pre_act):
    sigmoid_val = jax.nn.sigmoid(pre_act)
    return sigmoid_val * (1.0 + pre_act * (1.0 - sigmoid_val))


def feature_map(inputs, weight, block_len):
    head_count, head_width = (weight.shape[0], weight.shape[1])
    split_in = inputs.reshape(inputs.shape[0], head_count, head_width)
    pre_act = jnp.einsum("lhd,hde->hle", split_in, weight, preferred_element_type=jnp.float32)
    features_out = jax.nn.silu(pre_act).astype(jnp.bfloat16)
    return (pre_act, features_out.reshape(head_count, -1, block_len, head_width))


def heads_blocks(array, head_count, block_len):
    rows = array.shape[0]
    return array.reshape(rows // block_len, block_len, head_count, -1).transpose(2, 0, 1, 3)


def unblock(array):
    head_count, block_count, block_len, head_width = array.shape
    return array.transpose(1, 2, 0, 3).reshape(1, block_count * block_len, head_count * head_width)


def scan_forward(pair, identity):
    return prefix(pair, "ctx", combine, identity, False)


def scan_backward(pair, identity):
    return prefix(pair, "ctx", combine, identity, True)


def local(query, key, value, log_decay, grad_out, query_map, key_map):
    head_count, head_width = (query_map.shape[0], query_map.shape[1])
    tokens = query.shape[1]
    block_count = tokens // BLOCK
    out_scale = 1.0 / (head_width * math.sqrt(BLOCK))
    query_rows, key_rows = (query[0], key[0])
    pre_query, query_feat = feature_map(query_rows, query_map, BLOCK)
    pre_key, key_feat = feature_map(key_rows, key_map, BLOCK)
    value_heads = heads_blocks(value[0], head_count, BLOCK)
    grad_heads = heads_blocks(grad_out[0], head_count, BLOCK)
    cumulative = jnp.cumsum(log_decay[0].reshape(head_count, block_count, BLOCK), axis=-1)
    totals = cumulative[..., -1]
    decay_now = jnp.exp(totals)
    causal_mask = jnp.arange(BLOCK)[:, None] >= jnp.arange(BLOCK)[None, :]
    differ = cumulative[..., :, None] - cumulative[..., None, :]
    weights = jnp.where(causal_mask, jnp.exp(jnp.where(causal_mask, differ, 0.0)), 0.0)
    key_dec = (
        key_feat.astype(jnp.float32) * jnp.exp(totals[..., None] - cumulative)[..., None]
    ).astype(jnp.bfloat16)
    query_dec = (query_feat.astype(jnp.float32) * jnp.exp(cumulative)[..., None]).astype(
        jnp.bfloat16
    )
    updates = jnp.einsum(
        "hntd,hnte->hnde", key_dec, value_heads, preferred_element_type=jnp.float32
    )
    contribs = jnp.einsum(
        "hnsd,hnse->hnde", query_dec, grad_heads, preferred_element_type=jnp.float32
    )
    identity = (
        jnp.ones((head_count,), jnp.float32),
        jnp.zeros((head_count, head_width, head_width), jnp.float32),
    )
    device_pair = identity
    for block_index in range(block_count):
        device_pair = combine(device_pair, (decay_now[:, block_index], updates[:, block_index]))
    device_adjoint = identity
    for block_index in range(block_count - 1, -1, -1):
        device_adjoint = combine(
            device_adjoint, (decay_now[:, block_index], contribs[:, block_index])
        )
    local_list = [jnp.zeros((head_count, head_width, head_width), jnp.float32)]
    prior_list = [jnp.ones((head_count,), jnp.float32)]
    block_index = 0
    local_list.append(
        decay_now[:, block_index, None, None] * local_list[-1] + updates[:, block_index]
    )
    prior_list.append(prior_list[-1] * decay_now[:, block_index])
    local_states = jnp.stack(local_list, axis=1)
    prior_decay = jnp.stack(prior_list, axis=1)[:, :, None, None]
    incoming = scan_forward((device_pair[0], device_pair[1]), identity)
    entering = incoming[1]
    states = local_states + prior_decay * entering[:, None]
    state_round = states.astype(jnp.bfloat16)
    scores = jnp.einsum("hnsd,hntd->hnst", query_feat, key_feat, preferred_element_type=jnp.float32)
    block_probs = (scores * weights).astype(jnp.bfloat16)
    intra_out = jnp.einsum(
        "hnst,hntd->hnsd", block_probs, value_heads, preferred_element_type=jnp.float32
    )
    inter_out = jnp.einsum(
        "hnsd,hnde->hnse", query_dec, state_round, preferred_element_type=jnp.float32
    )
    output = (out_scale * (intra_out + inter_out)).astype(jnp.bfloat16)
    grad_scores = (
        jnp.einsum("hnse,hnte->hnst", grad_heads, value_heads, preferred_element_type=jnp.float32)
        * weights
    ).astype(jnp.bfloat16)
    grad_qfeat = out_scale * (
        jnp.einsum("hnst,hntd->hnsd", grad_scores, key_feat, preferred_element_type=jnp.float32)
        + jnp.exp(cumulative)[..., None]
        * jnp.einsum("hnse,hnde->hnsd", grad_heads, state_round, preferred_element_type=jnp.float32)
    )
    grad_pre_query = (
        grad_qfeat.reshape(head_count, tokens, head_width) * silu_slope(pre_query)
    ).astype(jnp.bfloat16)
    grad_query = jnp.einsum(
        "hle,hde->lhd", grad_pre_query, query_map, preferred_element_type=jnp.float32
    ).astype(jnp.bfloat16)
    query_part = jnp.einsum(
        "lhd,hle->hde",
        query_rows.reshape(tokens, head_count, head_width),
        grad_pre_query,
        preferred_element_type=jnp.float32,
    )
    outgoing = scan_backward((device_adjoint[0], device_adjoint[1]), identity)
    trailing = [outgoing[1]]
    block_index = 1
    trailing.insert(
        0, contribs[:, block_index] + decay_now[:, block_index, None, None] * trailing[0]
    )
    after_round = jnp.stack(trailing, axis=1).astype(jnp.bfloat16)
    grad_value = out_scale * (
        jnp.einsum("hnst,hnsd->hntd", block_probs, grad_heads, preferred_element_type=jnp.float32)
        + jnp.einsum("hntd,hnde->hnte", key_dec, after_round, preferred_element_type=jnp.float32)
    )
    grad_kfeat = out_scale * (
        jnp.einsum("hnst,hnsd->hntd", grad_scores, query_feat, preferred_element_type=jnp.float32)
        + jnp.exp(totals[..., None] - cumulative)[..., None]
        * jnp.einsum(
            "hnte,hnde->hntd", value_heads, after_round, preferred_element_type=jnp.float32
        )
    )
    grad_pre_key = (
        grad_kfeat.reshape(head_count, tokens, head_width) * silu_slope(pre_key)
    ).astype(jnp.bfloat16)
    grad_key = jnp.einsum(
        "hle,hde->lhd", grad_pre_key, key_map, preferred_element_type=jnp.float32
    ).astype(jnp.bfloat16)
    key_part = jnp.einsum(
        "lhd,hle->hde",
        key_rows.reshape(tokens, head_count, head_width),
        grad_pre_key,
        preferred_element_type=jnp.float32,
    )
    query_map_grad, key_map_grad = lax.psum((query_part, key_part), ("ctx", "dp"))
    return (
        unblock(output),
        grad_query.reshape(1, tokens, head_count * head_width),
        grad_key.reshape(1, tokens, head_count * head_width),
        unblock(grad_value.astype(jnp.bfloat16)),
        query_map_grad,
        key_map_grad,
    )


def solution(mesh):
    return jax.shard_map(
        local,
        mesh=mesh,
        in_specs=(
            P("dp", "ctx", None),
            P("dp", "ctx", None),
            P("dp", "ctx", None),
            P("dp", None, "ctx"),
            P("dp", "ctx", None),
            P(),
            P(),
        ),
        out_specs=(
            P("dp", "ctx", None),
            P("dp", "ctx", None),
            P("dp", "ctx", None),
            P("dp", "ctx", None),
            P(),
            P(),
        ),
        check_vma=False,
    )
```

profile of v0, /device:TPU:1, one launch (start us, length us, event | category | flops | bytes accessed | tf_op | source)
XLA Modules:
  0.0 339.0 jit_solution(6659050404977658721)
XLA Ops:
  9.8 1.5 copy.169
  11.6 2.0 multiply_convert_fusion.7
  18.3 19.0 %all-reduce.2 = f32[64]{0:T(128)S(1)} all-reduce(f32[64]{0:T(128)S(1)} %get-tuple-element.327), channel_id=2, replica_groups=mesh['ctx'=8,'dp'=4] {'ctx'}, use_global_device_ids=true, to_apply=%add.2 | all-reduce | flops 64 | bytes 512
  37.4 2.5 copy.170
  39.9 1.5 copy.171
  41.4 1.5 multiply_convert_fusion
  42.9 1.4 copy-done.6
  44.3 2.2 fusion.46
  46.5 46.3 %all-gather.6.cloned.1.call-done = f32[8,8,128,128]{3,2,1,0:T(8,128)} async-done(((f32[1,8,128,128]{3,2,1,0:T(8,128)}), f32[8,8,128,128]{3,2,1,0:T(8,128)}) %all-gather.6.cloned.1.call-update) | async-done | bytes 4194320 | tf_op jit(solution)/shard_map/all_gather | solution.py:13
  92.8 9.7 %while.31 = (s32[]{:T(128)}, f32[8,128,128]{2,1,0:T(8,128)S(1)}, s32[]{:T(128)}, f32[8,8]{1,0:T(8,128)S(1)}, f32[8,8,128,128]{3,2,1,0:T(8,128)}, /*index=5*/s32[]{:T(128)}, s32[]{:T(128)}, s32[]{:T(128)}, s32[]{:T(128)}) while((s32[]{:T(128)}, f32[8,128,128]{2,1,0:T(8,128)S(1)}, s32[]{:T(128)}, f32[8,8]{1,0:T(8,128)S(1)}, ...), condition=%wide.region_5.6_spmd.clone, body=%wide.region_4.5_spmd.clone.sunk | while | flops 524296 | bytes 1573135 | solution.py:26
  103.7 2.1 fusion.3
  105.8 2.3 fusion.2
  109.2 2.0 fusion.16
  113.4 2.7 multiply_convert_fusion.1
  119.1 1.6 copy.149
  120.8 2.3 reshape.165
  123.1 2.7 convolution_convert_fusion
  125.8 2.3 copy.155
  128.0 1.3 bitcast_add_fusion.7
  129.3 2.9 convolution_bitcast_fusion
  132.2 2.1 fusion.45
  134.4 2.1 fusion.18
  136.5 48.5 %all-gather.4.cloned.1.call-done = f32[8,8,128,128]{3,2,1,0:T(8,128)} async-done(((f32[1,8,128,128]{3,2,1,0:T(8,128)}), f32[8,8,128,128]{3,2,1,0:T(8,128)}) %all-gather.4.cloned.1.call-update) | async-done | bytes 4194320 | tf_op jit(solution)/shard_map/all_gather | solution.py:13
  185.0 9.7 %while.30 = (s32[]{:T(128)}, f32[8,128,128]{2,1,0:T(8,128)S(1)}, s32[]{:T(128)}, f32[8,8]{1,0:T(8,128)S(1)}, f32[8,8,128,128]{3,2,1,0:T(8,128)}, /*index=5*/s32[]{:T(128)}, s32[]{:T(128)}) while((s32[]{:T(128)}, f32[8,128,128]{2,1,0:T(8,128)S(1)}, s32[]{:T(128)}, f32[8,8]{1,0:T(8,128)S(1)}, f32[8,8,128,128]{3,2,1,0:T(8,128)}, ...), condition=%wide.region_3.4_spmd.clone, body=%wide.region_2.3_spmd.clone.sunk | while | flops 524292 | bytes 1573073 | solution.py:26
  194.7 2.2 fusion.5
  198.1 1.3 convolution_bitcast_fusion.1
  199.5 2.4 convolution_convert_fusion.1
  202.0 2.3 copy.154
  204.2 2.3 fusion.6
  208.5 119.9 %all-reduce.6.cloned.1.call-done = (f32[8,128,128]{1,2,0:T(8,128)}, f32[8,128,128]{1,2,0:T(8,128)}) async-done(((f32[8,128,128]{1,2,0:T(8,128)}, f32[8,128,128]{1,2,0:T(8,128)}), (f32[8,128,128]{1,2,0:T(8,128)}, f32[8,128,128]{1,2,0:T(8,128)})) %all-reduce.6.cloned.1.call-update) | async-done | bytes 1048592 | tf_op jit(solution)/shard_map/psum | solution.py:177
  328.4 2.0 copy.156
  330.4 2.0 copy.157
  (113 shorter events, 36.3 us)
Async XLA Ops:
  7.2 98.6 %copy-start = (bf16[8,128,128]{2,1,0:T(8,128)(2,1)S(1)}, bf16[8,128,128]{2,1,0:T(8,128)(2,1)}, u32[]{:S(2)}) copy-start(bf16[8,128,128]{2,1,0:T(8,128)(2,1)} %param.17) | copy-start | bytes 786436
  7.2 4.2 %copy-start.18 = (bf16[1,512,1024]{2,1,0:T(8,128)(2,1)S(1)}, bf16[1,512,1024]{2,1,0:T(8,128)(2,1)}, u32[]{:S(2)}) copy-start(bf16[1,512,1024]{2,1,0:T(8,128)(2,1)} %param.15) | copy-start | bytes 3145732
  7.2 85.6 %all-gather.6.cloned.1.call-start = ((), (), s32[]{:S(2)}) async-start(), calls=%async_computation.1 | async-start | bytes 4718592 | tf_op jit(solution)/shard_map/all_gather | solution.py:13
  9.8 1.9 copy-start.19
  11.3 2.3 copy-start.14
  13.6 2.6 copy-start.12
  13.6 0.7 copy-start.20
  14.2 4.0 %copy-start.4 = (bf16[8,2,256,128]{2,3,1,0:T(8,128)(2,1)}, bf16[8,2,256,128]{2,3,1,0:T(8,128)(2,1)S(1)}, u32[]{:S(2)}) copy-start(bf16[8,2,256,128]{2,3,1,0:T(8,128)(2,1)S(1)} %copy.130) | copy-start | bytes 3145732
  16.3 1.0 copy-start.10
  18.2 166.8 %all-gather.4.cloned.1.call-start = ((), (), s32[]{:S(2)}) async-start(), calls=%async_computation | async-start | bytes 4718592 | tf_op jit(solution)/shard_map/all_gather | solution.py:13
  41.4 2.9 copy-start.13
  42.9 1.4 copy-start.6
  103.7 2.1 copy-start.16
  108.1 1.1 copy-start.1
  111.2 1.0 copy-start.11
  113.2 215.2 %all-reduce.6.cloned.1.call-start = ((), (), s32[]{:S(2)}) async-start(), calls=%async_computation.2 | async-start | bytes 2097152 | tf_op jit(solution)/shard_map/psum | solution.py:177
  116.2 1.3 copy-start.8
  116.2 2.0 copy-start.2
  128.0 4.2 %copy-start.3 = (bf16[8,512,128]{2,1,0:T(8,128)(2,1)S(1)}, bf16[8,512,128]{2,1,0:T(8,128)(2,1)}, u32[]{:S(2)}) copy-start(bf16[8,512,128]{2,1,0:T(8,128)(2,1)} %copy-done.1) | copy-start | bytes 3145732
  128.0 4.2 %copy-start.7 = (bf16[8,2,256,256]{3,2,1,0:T(8,128)(2,1)S(1)}, bf16[8,2,256,256]{3,2,1,0:T(8,128)(2,1)}, u32[]{:S(2)}) copy-start(bf16[8,2,256,256]{3,2,1,0:T(8,128)(2,1)} %copy-done.6) | copy-start | bytes 6291460
  132.2 2.1 copy-start.9
  194.7 2.2 copy-start.17
  196.9 1.2 copy-start.15
  199.5 4.7 %copy-start.5 = (bf16[8,2,256,128]{2,3,1,0:T(8,128)(2,1)S(1)}, bf16[8,2,256,128]{2,3,1,0:T(8,128)(2,1)}, u32[]{:S(2)}) copy-start(bf16[8,2,256,128]{2,3,1,0:T(8,128)(2,1)} %copy-done.4) | copy-start | bytes 3145732
Sparse Core Ops, SparseCore 0:
  18.3 74.4 all-gather.5
  113.3 71.6 all-gather.3
  199.6 128.7 all-reduce.5
where the time goes:
time: 342 us; the launch traced here: 339 us
  waiting for transfers between devices  215 us (63%)
  matrix products  35.1 us (10%)
  local copies, waits for them, and re-layouts  29.2 us (9%)
  other arithmetic  25.4 us (7%)
  blocking collectives  19 us (6%)
  between operations  14.8 us (4%)
    psum x1, waiting for transfers between devices, local(): lax.psum((query_part, key_part), ('ctx', 'dp'))  120 us
    all_gather x2, waiting for transfers between devices, prefix(): everything = jax.tree.map(lambda part: lax.all_gather(part, axis), value)  94.8 us
    unnamed x52, local copies, waits for them, and re-layouts  21.3 us
    unnamed x1, blocking collectives  19 us
    select_n x16, other arithmetic, step(): return jax.tree.map(lambda a, b: jnp.where(reached, a, b), new, before)  18.8 us
  transfers between devices with their start and end apart: 3, of which 3 were waited for; matrix products, arithmetic and copies ran while one was open for 11% of the time, Pallas kernels for 0%

commit v1 on v0

v1 whole, which is shorter than its diff:
```python
import functools
import math

import jax
import jax.numpy as jnp
from jax import lax
from jax.experimental import pallas as pl
from jax.experimental.pallas import tpu as pltpu
from jax.sharding import PartitionSpec as P

BLOCK = 256
MESH = pl.DeviceIdType.MESH
F32 = jnp.float32
BF16 = jnp.bfloat16


def mm(a, b):
    return lax.dot_general(a, b, (((1,), (0,)), ((), ())), preferred_element_type=F32)


def mm_nt(a, b):
    return lax.dot_general(a, b, (((1,), (1,)), ((), ())), preferred_element_type=F32)


def mm_tn(a, b):
    return lax.dot_general(a, b, (((0,), (0,)), ((), ())), preferred_element_type=F32)


def sigmoid(u):
    return 1.0 / (1.0 + jnp.exp(-u))


def kernel(
    n, nd, heads, width, tokens,
    q_h, k_h, v_h, ld_ref, g_h, qm_ref, km_ref,
    o_h, gq_h, gk_h, gv_h, res_h,
    q_s, k_s, v_s, g_s, o_s, gq_s, gk_s, gv_s,
    preq_s, prek_s, qf_s, kf_s, qd_s, kd_s,
    cum_s, col_s, mine_s, theirs_s,
    U_s, C_s, u0_s, c1_s, fin_s, fout_s, xout_s, xin_s,
    part_s, pin_s, own_s, cin_s, res_s,
    in_sem, out_sem, dec_sem, ch_send, ch_recv, x_send, x_recv,
    p_send, p_recv, c_send, c_recv, ag_send, ag_recv,
    y_send, y_recv, k_send, k_recv,
):
    scale = 1.0 / (width * math.sqrt(BLOCK))
    me = lax.axis_index("ctx")
    d = lax.axis_index("dp")
    nz = n // 2
    z = me // 2
    x = lax.rem(me, 2)
    partner = me + 1 - 2 * x
    rows = width // nd

    loads = [
        pltpu.make_async_copy(src, dst, in_sem.at[i])
        for i, (src, dst) in enumerate(((k_h, k_s), (v_h, v_s), (q_h, q_s), (g_h, g_s)))
    ]
    for copy in loads:
        copy.start()

    barrier = pltpu.get_barrier_semaphore()

    @pl.loop(1, n)
    def _(r):
        pl.semaphore_signal(
            barrier, inc=1, device_id=(lax.rem(me + r, n), d), device_id_type=MESH
        )

    for r in range(1, nd):
        pl.semaphore_signal(
            barrier, inc=1, device_id=(me, lax.rem(d + r, nd)), device_id_type=MESH
        )

    cum = ld_ref[...]
    lane = lax.rem(lax.broadcasted_iota(jnp.int32, cum.shape, 1), BLOCK)
    shift = 1
    while shift < BLOCK:
        cum = cum + jnp.where(lane >= shift, pltpu.roll(cum, shift, 1), 0.0)
        shift *= 2
    cum_s[...] = cum
    last = cum[:, BLOCK - 1 : BLOCK] + cum[:, 2 * BLOCK - 1 : 2 * BLOCK]
    mine_s[...] = jnp.broadcast_to(last, mine_s.shape)

    @pl.when(z == 0)
    def _():
        fin_s[0] = jnp.zeros_like(fin_s[0])

    @pl.when(z == nz - 1)
    def _():
        fin_s[1] = jnp.zeros_like(fin_s[1])

    pl.semaphore_wait(barrier, n - 1 + nd - 1)
    decay_copy = pltpu.make_async_remote_copy(
        src_ref=mine_s, dst_ref=theirs_s, send_sem=dec_sem.at[0], recv_sem=dec_sem.at[1],
        device_id=(partner, d), device_id_type=MESH,
    )
    decay_copy.start()
    for copy in loads:
        copy.wait()
    decay_copy.wait()

    def cols(h):
        return pl.ds(pl.multiple_of(h * width, width), width)

    def blk(b):
        return pl.ds(b * BLOCK, BLOCK)

    def first_pass(h):
        c = cols(h)
        pre = mm(k_s[:, c], km_ref[h])
        prek_s[:, c] = pre
        kf_s[:, c] = (pre * sigmoid(pre)).astype(BF16)
        pre = mm(q_s[:, c], qm_ref[h])
        preq_s[:, c] = pre
        qf_s[:, c] = (pre * sigmoid(pre)).astype(BF16)
        col = jnp.broadcast_to(cum_s[pl.ds(h, 1), :], (width, tokens)).T
        col_s[h] = col
        u, w = [], []
        for b in range(2):
            cb = col[b * BLOCK : (b + 1) * BLOCK]
            tot = cb[BLOCK - 1 : BLOCK]
            kd = (kf_s[blk(b), c].astype(F32) * jnp.exp(tot - cb)).astype(BF16)
            kd_s[blk(b), c] = kd
            u.append(mm_tn(kd, v_s[blk(b), c]))
            qd = (qf_s[blk(b), c].astype(F32) * jnp.exp(cb)).astype(BF16)
            qd_s[blk(b), c] = qd
            w.append(mm_tn(qd, g_s[blk(b), c]))
        d0 = jnp.exp(col[BLOCK - 1 : BLOCK])
        d1 = jnp.exp(col[2 * BLOCK - 1 : 2 * BLOCK])
        U_s[h] = d1 * u[0] + u[1]
        u0_s[h] = u[0]
        C_s[h] = w[0] + d0 * w[1]
        c1_s[h] = w[1]

    def chain_copy(way, h):
        to = z + 1 if way == 0 else z - 1
        to = jnp.clip(to, 0, nz - 1) * 2 + x
        return pltpu.make_async_remote_copy(
            src_ref=fout_s.at[way, h], dst_ref=fin_s.at[way, h],
            send_sem=ch_send.at[way, h], recv_sem=ch_recv.at[way, h],
            device_id=(to, d), device_id_type=MESH,
        )

    def cross_copy(way, h):
        return pltpu.make_async_remote_copy(
            src_ref=xout_s.at[way, h], dst_ref=xin_s.at[way, h],
            send_sem=x_send.at[way, h], recv_sem=x_recv.at[way, h],
            device_id=(partner, d), device_id_type=MESH,
        )

    def is_first(way):
        return (x == 0) if way == 0 else (x == 1)

    def has_in(way):
        return (z > 0) if way == 0 else (z < nz - 1)

    def has_out(way):
        return (z < nz - 1) if way == 0 else (z > 0)

    def chain(way, h):
        @pl.when(has_in(way))
        def _():
            chain_copy(way, h).wait_recv()

        own = mine_s[pl.ds(h, 1), :]
        other = theirs_s[pl.ds(h, 1), :]
        state = fin_s[way, h]
        term = (U_s if way == 0 else C_s)[h]
        first = is_first(way)

        @pl.when(has_out(way))
        def _():
            carry = jnp.where(first, jnp.exp(other), 1.0)
            fout_s[way, h] = jnp.exp(own + other) * state + carry * term
            chain_copy(way, h).start()

        keep = jnp.where(first, jnp.exp(own), 1.0)
        xout_s[way, h] = keep * state + jnp.where(first, term, 0.0)
        cross_copy(way, h).start()

    def entering(way, h):
        cross_copy(way, h).wait_recv()
        other = theirs_s[pl.ds(h, 1), :]
        keep = jnp.where(is_first(way), 1.0, jnp.exp(other))
        return keep * fin_s[way, h] + xin_s[way, h]

    def part_copy(m, r):
        to = lax.rem(d + r, nd)
        return pltpu.make_async_remote_copy(
            src_ref=part_s.at[to, m], dst_ref=pin_s.at[r - 1, m],
            send_sem=p_send.at[r - 1, m], recv_sem=p_recv.at[r - 1, m],
            device_id=(me, to), device_id_type=MESH,
        )

    def send_part(m, part):
        for i in range(nd):
            part_s[i, m] = part[i * rows : (i + 1) * rows]
        for r in range(1, nd):
            part_copy(m, r).start()

    iota0 = lax.broadcasted_iota(jnp.int32, (BLOCK, BLOCK), 0)
    iota1 = lax.broadcasted_iota(jnp.int32, (BLOCK, BLOCK), 1)

    def wide(cb):
        return jnp.concatenate([cb] * (BLOCK // width), axis=1)

    def slope(pre):
        s = sigmoid(pre)
        return s * (1.0 + pre * (1.0 - s))

    def finish_q(h):
        c = cols(h)
        state = entering(0, h)
        d0 = jnp.exp(col_s[h, pl.ds(BLOCK - 1, 1), :])
        states = (state.astype(BF16), (d0 * state + u0_s[h]).astype(BF16))
        total = None
        for b in range(2):
            st = states[b]
            cb = col_s[h, blk(b), :]
            row = cum_s[pl.ds(h, 1), blk(b)]
            weight = jnp.exp(jnp.where(iota0 >= iota1, wide(cb) - row, -1e30))
            kf, v, g = kf_s[blk(b), c], v_s[blk(b), c], g_s[blk(b), c]
            probs = (mm_nt(qf_s[blk(b), c], kf) * weight).astype(BF16)
            o_s[blk(b), c] = (scale * (mm(probs, v) + mm(qd_s[blk(b), c], st))).astype(BF16)
            gs = (mm_nt(g, v) * weight).astype(BF16)
            gf = scale * (mm(gs, kf) + jnp.exp(cb) * mm_nt(g, st))
            gp = (gf * slope(preq_s[blk(b), c])).astype(BF16)
            gq_s[blk(b), c] = mm_nt(gp, qm_ref[h]).astype(BF16)
            p = mm_tn(q_s[blk(b), c], gp)
            total = p if total is None else total + p
        send_part(h, total)

    def finish_k(h):
        c = cols(h)
        after = entering(1, h)
        d1 = jnp.exp(col_s[h, pl.ds(2 * BLOCK - 1, 1), :])
        afters = ((c1_s[h] + d1 * after).astype(BF16), after.astype(BF16))
        total = None
        for b in range(2):
            af = afters[b]
            cb = col_s[h, blk(b), :]
            tot = cb[BLOCK - 1 : BLOCK]
            row = cum_s[pl.ds(h, 1), blk(b)]
            weight = jnp.exp(jnp.where(iota1 >= iota0, row - wide(cb), -1e30))
            qf, v, g = qf_s[blk(b), c], v_s[blk(b), c], g_s[blk(b), c]
            probs = (mm_nt(kf_s[blk(b), c], qf) * weight).astype(BF16)
            gv_s[blk(b), c] = (scale * (mm(probs, g) + mm(kd_s[blk(b), c], af))).astype(BF16)
            gs = (mm_nt(v, g) * weight).astype(BF16)
            gf = scale * (mm(gs, qf) + jnp.exp(tot - cb) * mm_nt(v, af))
            gp = (gf * slope(prek_s[blk(b), c])).astype(BF16)
            gk_s[blk(b), c] = mm_nt(gp, km_ref[h]).astype(BF16)
            p = mm_tn(k_s[blk(b), c], gp)
            total = p if total is None else total + p
        send_part(heads + h, total)

    def inside(h):
        return jnp.logical_and(h >= 0, h < heads)

    @pl.loop(0, heads + 2 * (nz - 1) + 2)
    def _(s):
        hf = s - 2 * z
        ha = s - 2 * (nz - 1 - z)

        @pl.when(s < heads)
        def _():
            first_pass(s)

        @pl.when(inside(hf))
        def _():
            chain(0, hf)

        @pl.when(inside(ha))
        def _():
            chain(1, ha)

        @pl.when(inside(hf - 2))
        def _():
            finish_q(hf - 2)

        @pl.when(inside(ha - 2))
        def _():
            finish_k(ha - 2)

    stores = [
        pltpu.make_async_copy(src, dst, out_sem.at[i])
        for i, (src, dst) in enumerate(((o_s, o_h), (gq_s, gq_h), (gk_s, gk_h), (gv_s, gv_h)))
    ]
    for copy in stores:
        copy.start()

    @pl.loop(0, 2 * heads)
    def _(m):
        total = part_s[d, m]
        for r in range(1, nd):
            part_copy(m, r).wait_recv()
            total = total + pin_s[r - 1, m]
        own_s[pl.ds(pl.multiple_of(m * rows, rows), rows), :] = total

    size = own_s.shape[0] // n

    def piece(i):
        return pl.ds(pl.multiple_of(i * size, size), size)

    def ctx_copy(r):
        to = lax.rem(me + r, n)
        return pltpu.make_async_remote_copy(
            src_ref=own_s.at[piece(to)], dst_ref=cin_s.at[r - 1],
            send_sem=c_send.at[r - 1], recv_sem=c_recv.at[r - 1],
            device_id=(to, d), device_id_type=MESH,
        )

    @pl.loop(1, n)
    def _(r):
        ctx_copy(r).start()

    res_s[d, piece(me)] = own_s[piece(me)]

    @pl.loop(1, n)
    def _(r):
        ctx_copy(r).wait_recv()
        res_s[d, piece(me)] = res_s[d, piece(me)] + cin_s[r - 1]

    def gather_copy(r):
        return pltpu.make_async_remote_copy(
            src_ref=res_s.at[d, piece(me)], dst_ref=res_s.at[d, piece(me)],
            send_sem=ag_send.at[r - 1], recv_sem=ag_recv.at[r - 1],
            device_id=(lax.rem(me + r, n), d), device_id_type=MESH,
        )

    def gather_arrival(r):
        at = piece(lax.rem(me + n - r, n))
        return pltpu.make_async_remote_copy(
            src_ref=res_s.at[d, at], dst_ref=res_s.at[d, at],
            send_sem=ag_send.at[r - 1], recv_sem=ag_recv.at[r - 1],
            device_id=(lax.rem(me + r, n), d), device_id_type=MESH,
        )

    across = lax.rem(d + 2, nd)
    beside = d + 1 - 2 * lax.rem(d, 2)
    diagonal = lax.rem(beside + 2, nd)

    def y_copy(r, whose):
        at = piece(lax.rem(me + n - r, n))
        return pltpu.make_async_remote_copy(
            src_ref=res_s.at[whose, at], dst_ref=res_s.at[whose, at],
            send_sem=y_send.at[r], recv_sem=y_recv.at[r],
            device_id=(me, across), device_id_type=MESH,
        )

    def core_copy(r, i, whose):
        at = piece(lax.rem(me + n - r, n))
        return pltpu.make_async_remote_copy(
            src_ref=res_s.at[whose, at], dst_ref=res_s.at[whose, at],
            send_sem=k_send.at[i, r], recv_sem=k_recv.at[i, r],
            device_id=(me, beside), device_id_type=MESH,
        )

    @pl.loop(1, n)
    def _(r):
        gather_copy(r).start()

    @pl.loop(0, n)
    def _(r):
        @pl.when(r > 0)
        def _():
            gather_arrival(r).wait_recv()

        y_copy(r, d).start()
        core_copy(r, 0, d).start()

    @pl.loop(0, n)
    def _(r):
        y_copy(r, across).wait_recv()
        core_copy(r, 1, across).start()

    @pl.loop(0, n)
    def _(r):
        core_copy(r, 0, beside).wait_recv()
        core_copy(r, 1, diagonal).wait_recv()

    result = pltpu.make_async_copy(res_s, res_h, out_sem.at[4])
    result.start()

    @pl.loop(0, heads)
    def _(h):
        for way in range(2):
            cross_copy(way, h).wait_send()

            @pl.when(has_out(way))
            def _():
                chain_copy(way, h).wait_send()

    @pl.loop(0, 2 * heads)
    def _(m):
        for r in range(1, nd):
            part_copy(m, r).wait_send()

    @pl.loop(1, n)
    def _(r):
        ctx_copy(r).wait_send()
        gather_copy(r).wait_send()

    @pl.loop(0, n)
    def _(r):
        y_copy(r, d).wait_send()
        core_copy(r, 0, d).wait_send()
        core_copy(r, 1, across).wait_send()

    for copy in stores:
        copy.wait()
    result.wait()


def solution(mesh):
    n, nd = mesh.shape["ctx"], mesh.shape["dp"]

    def local(query, key, value, log_decay, grad_out, query_map, key_map):
        heads, width = query_map.shape[0], query_map.shape[1]
        tokens = query.shape[1]
        wide = heads * width
        rows = width // nd
        owned = 2 * heads * rows
        any_spec = pl.BlockSpec(memory_space=pl.ANY)
        vmem_spec = pl.BlockSpec(memory_space=pltpu.VMEM)
        act = pltpu.VMEM((tokens, wide), BF16)
        act32 = pltpu.VMEM((tokens, wide), F32)
        mats = pltpu.VMEM((heads, width, width), F32)
        mats2 = pltpu.VMEM((2, heads, width, width), F32)
        dma = pltpu.SemaphoreType.DMA
        outs = pl.pallas_call(
            functools.partial(kernel, n, nd, heads, width, tokens),
            out_shape=[jax.ShapeDtypeStruct((tokens, wide), BF16)] * 4
            + [jax.ShapeDtypeStruct((nd, owned, width), F32)],
            in_specs=[any_spec, any_spec, any_spec, vmem_spec, any_spec, vmem_spec, vmem_spec],
            out_specs=[any_spec] * 5,
            scratch_shapes=[act] * 8
            + [act32] * 2
            + [act] * 4
            + [
                pltpu.VMEM((heads, tokens), F32),
                pltpu.VMEM((heads, tokens, width), F32),
                pltpu.VMEM((heads, width), F32),
                pltpu.VMEM((heads, width), F32),
            ]
            + [mats] * 4
            + [mats2] * 4
            + [
                pltpu.VMEM((nd, 2 * heads, rows, width), F32),
                pltpu.VMEM((nd - 1, 2 * heads, rows, width), F32),
                pltpu.VMEM((owned, width), F32),
                pltpu.VMEM((n - 1, owned // n, width), F32),
                pltpu.VMEM((nd, owned, width), F32),
            ]
            + [
                dma((4,)),
                dma((5,)),
                dma((2,)),
                dma((2, heads)),
                dma((2, heads)),
                dma((2, heads)),
                dma((2, heads)),
                dma((nd - 1, 2 * heads)),
                dma((nd - 1, 2 * heads)),
                dma((n - 1,)),
                dma((n - 1,)),
                dma((n - 1,)),
                dma((n - 1,)),
                dma((n,)),
                dma((n,)),
                dma((2, n)),
                dma((2, n)),
            ],
            compiler_params=pltpu.CompilerParams(
                collective_id=0, has_side_effects=True, vmem_limit_bytes=48 * 1024 * 1024
            ),
            cost_estimate=pl.CostEstimate(
                flops=4_000_000_000, bytes_accessed=10_000_000, transcendentals=4_000_000
            ),
        )(query[0], key[0], value[0], log_decay[0], grad_out[0], query_map, key_map)
        maps = outs[4].reshape(nd, 2, heads, rows, width).transpose(1, 2, 0, 3, 4)
        maps = maps.reshape(2, heads, width, width)
        return (outs[0][None], outs[1][None], outs[2][None], outs[3][None], maps[0], maps[1])

    return jax.shard_map(
        local,
        mesh=mesh,
        in_specs=(
            P("dp", "ctx", None),
            P("dp", "ctx", None),
            P("dp", "ctx", None),
            P("dp", None, "ctx"),
            P("dp", "ctx", None),
            P(),
            P(),
        ),
        out_specs=(
            P("dp", "ctx", None),
            P("dp", "ctx", None),
            P("dp", "ctx", None),
            P("dp", "ctx", None),
            P(),
            P(),
        ),
        check_vma=False,
    )
```

time: 342 us -> 74.2 us (0.22)
  waiting for transfers between devices: 215 us -> 0 us
  Pallas kernels: 0 us -> 65 us
  matrix products: 35.1 us -> 0 us
  other arithmetic: 25.4 us -> 0 us
  local copies, waits for them, and re-layouts: 29.2 us -> 8.27 us
  blocking collectives: 19 us -> 0 us
  between operations: 14.8 us -> 0.66 us
    psum x1 -> x0, waiting for transfers between devices: 120 us -> none  [local(): lax.psum((query_part, key_part), ('ctx', 'dp'))]
    all_gather x2 -> x0, waiting for transfers between devices: 94.8 us -> none  [prefix(): everything = jax.tree.map(lambda part: lax.all_gather(part, axis), value)]
    pallas_call x0 -> x1, Pallas kernels: none -> 65 us  [local(): pl.pallas_call(functools.partial(kernel, n, nd, heads, width, tokens), ou...]
    dot_general x18 -> x0, matrix products: 35.1 us -> none  [the longest x2 4.28 us: feature_map(): jnp.einsum('lhd,hde->hle', split_in, weight, preferred_element_type=jnp.f...]
    unnamed x1 -> x0, blocking collectives: 19 us -> none
    select_n x16 -> x0, other arithmetic: 18.8 us -> none  [step(): return jax.tree.map(lambda a, b: jnp.where(reached, a, b), new, before)]
    unnamed x52 -> x10, local copies, waits for them, and re-layouts: 21.3 us -> 6.49 us
    reshape x4 -> x0, local copies, waits for them, and re-layouts: 4.94 us -> none  [the longest x2 3.61 us: unblock(): array.transpose(1, 2, 0, 3)]
  transfers between devices with their start and end apart: 3 -> 0, of which waited for: 3 -> 0; matrix products, arithmetic and copies ran while one was open for 11% -> 0% of each run, Pallas kernels for 0% -> 0%
where the time goes in v1:
time: 74.2 us; the launch traced here: 73.9 us
  Pallas kernels  65 us (88%)
  local copies, waits for them, and re-layouts  8.27 us (11%)
    pallas_call x1, Pallas kernels, local(): pl.pallas_call(functools.partial(kernel, n, nd, heads, width, tokens), ou...  65 us
    unnamed x10, local copies, waits for them, and re-layouts  6.49 us

profile of v1, /device:TPU:1, one launch (start us, length us, event | category | flops | bytes accessed | tf_op | source)
XLA Modules:
  0.0 73.9 jit_solution(10004208110339710321)
XLA Ops:
  0.6 0.0 copy-start
  0.6 0.9 %copy-done = bf16[8,128,128]{2,1,0:T(8,128)(2,1)S(1)} copy-done((bf16[8,128,128]{2,1,0:T(8,128)(2,1)S(1)}, bf16[8,128,128]{2,1,0:T(8,128)(2,1)}, u32[]{:S(2)}) %copy-start) | copy-done | bytes 262168
  1.6 0.0 copy-start.1
  1.6 0.9 %copy-done.1 = bf16[8,128,128]{2,1,0:T(8,128)(2,1)S(1)} copy-done((bf16[8,128,128]{2,1,0:T(8,128)(2,1)S(1)}, bf16[8,128,128]{2,1,0:T(8,128)(2,1)}, u32[]{:S(2)}) %copy-start.1) | copy-done | bytes 262168
  2.5 0.0 copy-start.2
  2.5 0.7 copy-done.2
  3.3 65.0 %shard_map.118 = (bf16[512,1024]{1,0:T(8,128)(2,1)S(1)}, bf16[512,1024]{1,0:T(8,128)(2,1)S(1)}, bf16[512,1024]{1,0:T(8,128)(2,1)S(1)}, bf16[512,1024]{1,0:T(8,128)(2,1)S(1)}, f32[4,512,128]{2,1,0:T(8,128)S(1)}) custom-call(bf16[512,1024]{1,0:T(8,128)(2,1)} %bitcast.22, bf16[512,1024]{1,0:T(8,128)(2,1)} %bitcast.23, bf16[512,1024]{1,0:T(8,128)(2,1)} %bitcast.24, ...), custom_call_target="tpu_custom_call" | custom-call | flops 4000000000 | bytes 10000000 | tf_op jit(solution)/shard_map/pallas_call | solution.py:431
  68.2 0.1 fusion
  68.4 0.8 %copy.14 = f32[1,8,4,32,128]{4,3,2,1,0:T(8,128)} copy(f32[1,8,4,32,128]{4,3,1,0,2:T(8,128)S(1)} %get-tuple-element.16) | data formatting | bytes 1048576 | tf_op jit(solution)/shard_map/slice | solution.py:483
  69.2 0.8 %copy.13 = f32[1,8,4,32,128]{4,3,2,1,0:T(8,128)} copy(f32[1,8,4,32,128]{4,3,1,0,2:T(8,128)S(1)} %get-tuple-element.17) | data formatting | bytes 1048576 | tf_op jit(solution)/shard_map/slice | solution.py:483
  70.0 1.0 %copy.19 = bf16[1,512,1024]{2,1,0:T(8,128)(2,1)} copy(bf16[1,512,1024]{2,1,0:T(8,128)(2,1)S(1)} %bitcast.17) | data formatting | bytes 2097152
  71.0 1.0 %copy.20 = bf16[1,512,1024]{2,1,0:T(8,128)(2,1)} copy(bf16[1,512,1024]{2,1,0:T(8,128)(2,1)S(1)} %bitcast.16) | data formatting | bytes 2097152
  72.0 1.0 %copy.21 = bf16[1,512,1024]{2,1,0:T(8,128)(2,1)} copy(bf16[1,512,1024]{2,1,0:T(8,128)(2,1)S(1)} %bitcast.15) | data formatting | bytes 2097152
  72.9 1.0 %copy.22 = bf16[1,512,1024]{2,1,0:T(8,128)(2,1)} copy(bf16[1,512,1024]{2,1,0:T(8,128)(2,1)S(1)} %bitcast.14) | data formatting | bytes 2097152
Async XLA Ops:
  0.6 1.0 %copy-start = (bf16[8,128,128]{2,1,0:T(8,128)(2,1)S(1)}, bf16[8,128,128]{2,1,0:T(8,128)(2,1)}, u32[]{:S(2)}) copy-start(bf16[8,128,128]{2,1,0:T(8,128)(2,1)} %qm_ref.1) | copy-start | bytes 786436
  1.6 0.9 %copy-start.1 = (bf16[8,128,128]{2,1,0:T(8,128)(2,1)S(1)}, bf16[8,128,128]{2,1,0:T(8,128)(2,1)}, u32[]{:S(2)}) copy-start(bf16[8,128,128]{2,1,0:T(8,128)(2,1)} %km_ref.1) | copy-start | bytes 786436
  2.5 0.7 copy-start.2

commit v2 on v1

--- a/solution.py
+++ b/solution.py
@@ -31,12 +31,12 @@
 
 
 def kernel(
-    n, nd, heads, width, tokens,
+    n, nd, groups, heads, width, tokens,
     q_h, k_h, v_h, ld_ref, g_h, qm_ref, km_ref,
     o_h, gq_h, gk_h, gv_h, res_h,
     q_s, k_s, v_s, g_s, o_s, gq_s, gk_s, gv_s,
-    preq_s, prek_s, qf_s, kf_s, qd_s, kd_s,
-    cum_s, col_s, mine_s, theirs_s,
+    sq_s, sk_s, qf_s, kf_s, qd_s, kd_s,
+    cum_s, col_s, eq_s, ek_s, mine_s, theirs_s,
     U_s, C_s, u0_s, c1_s, fin_s, fout_s, xout_s, xin_s,
     part_s, pin_s, own_s, cin_s, res_s,
     in_sem, out_sem, dec_sem, ch_send, ch_recv, x_send, x_recv,
@@ -51,6 +51,7 @@
     x = lax.rem(me, 2)
     partner = me + 1 - 2 * x
     rows = width // nd
+    hh = heads // groups
 
     loads = [
         pltpu.make_async_copy(src, dst, in_sem.at[i])
@@ -109,21 +110,30 @@
     def first_pass(h):
         c = cols(h)
         pre = mm(k_s[:, c], km_ref[h])
-        prek_s[:, c] = pre
-        kf_s[:, c] = (pre * sigmoid(pre)).astype(BF16)
+        sig = sigmoid(pre)
+        sk_s[:, c] = sig * (1.0 + pre * (1.0 - sig))
+        kf = (pre * sig).astype(BF16)
+        kf_s[:, c] = kf
         pre = mm(q_s[:, c], qm_ref[h])
-        preq_s[:, c] = pre
-        qf_s[:, c] = (pre * sigmoid(pre)).astype(BF16)
+        sig = sigmoid(pre)
+        sq_s[:, c] = sig * (1.0 + pre * (1.0 - sig))
+        qf = (pre * sig).astype(BF16)
+        qf_s[:, c] = qf
         col = jnp.broadcast_to(cum_s[pl.ds(h, 1), :], (width, tokens)).T
         col_s[h] = col
         u, w = [], []
         for b in range(2):
             cb = col[b * BLOCK : (b + 1) * BLOCK]
             tot = cb[BLOCK - 1 : BLOCK]
-            kd = (kf_s[blk(b), c].astype(F32) * jnp.exp(tot - cb)).astype(BF16)
+            part = slice(b * BLOCK, (b + 1) * BLOCK)
+            ek = jnp.exp(tot - cb)
+            eq = jnp.exp(cb)
+            ek_s[h, blk(b), :] = ek
+            eq_s[h, blk(b), :] = eq
+            kd = (kf[part].astype(F32) * ek).astype(BF16)
             kd_s[blk(b), c] = kd
             u.append(mm_tn(kd, v_s[blk(b), c]))
-            qd = (qf_s[blk(b), c].astype(F32) * jnp.exp(cb)).astype(BF16)
+            qd = (qf[part].astype(F32) * eq).astype(BF16)
             qd_s[blk(b), c] = qd
             w.append(mm_tn(qd, g_s[blk(b), c]))
         d0 = jnp.exp(col[BLOCK - 1 : BLOCK])
@@ -199,15 +209,16 @@
         for r in range(1, nd):
             part_copy(m, r).start()
 
-    iota0 = lax.broadcasted_iota(jnp.int32, (BLOCK, BLOCK), 0)
-    iota1 = lax.broadcasted_iota(jnp.int32, (BLOCK, BLOCK), 1)
-
-    def wide(cb):
-        return jnp.concatenate([cb] * (BLOCK // width), axis=1)
-
-    def slope(pre):
-        s = sigmoid(pre)
-        return s * (1.0 + pre * (1.0 - s))
+    half = BLOCK // 2
+    iota0 = lax.broadcasted_iota(jnp.int32, (half, half), 0)
+    iota1 = lax.broadcasted_iota(jnp.int32, (half, half), 1)
+    low, high = slice(0, half), slice(half, BLOCK)
+
+    def stack(a, b, axis):
+        return jnp.concatenate([a, b], axis=axis)
+
+    def masked_exp(keep, value):
+        return jnp.exp(jnp.where(keep, value, -1e30))
 
     def finish_q(h):
         c = cols(h)
@@ -219,17 +230,26 @@
             st = states[b]
             cb = col_s[h, blk(b), :]
             row = cum_s[pl.ds(h, 1), blk(b)]
-            weight = jnp.exp(jnp.where(iota0 >= iota1, wide(cb) - row, -1e30))
-            kf, v, g = kf_s[blk(b), c], v_s[blk(b), c], g_s[blk(b), c]
-            probs = (mm_nt(qf_s[blk(b), c], kf) * weight).astype(BF16)
-            o_s[blk(b), c] = (scale * (mm(probs, v) + mm(qd_s[blk(b), c], st))).astype(BF16)
-            gs = (mm_nt(g, v) * weight).astype(BF16)
-            gf = scale * (mm(gs, kf) + jnp.exp(cb) * mm_nt(g, st))
-            gp = (gf * slope(preq_s[blk(b), c])).astype(BF16)
+            w0 = masked_exp(iota0 >= iota1, cb[low] - row[:, low])
+            w1 = stack(
+                jnp.exp(cb[high] - row[:, low]),
+                masked_exp(iota0 >= iota1, cb[high] - row[:, high]),
+                1,
+            )
+            qf, kf, v, g = qf_s[blk(b), c], kf_s[blk(b), c], v_s[blk(b), c], g_s[blk(b), c]
+            p0 = (mm_nt(qf[low], kf[low]) * w0).astype(BF16)
+            p1 = (mm_nt(qf[high], kf) * w1).astype(BF16)
+            intra = stack(mm(p0, v[low]), mm(p1, v), 0)
+            o_s[blk(b), c] = (scale * (intra + mm(qd_s[blk(b), c], st))).astype(BF16)
+            g0 = (mm_nt(g[low], v[low]) * w0).astype(BF16)
+            g1 = (mm_nt(g[high], v) * w1).astype(BF16)
+            intra = stack(mm(g0, kf[low]), mm(g1, kf), 0)
+            gf = scale * (intra + eq_s[h, blk(b), :] * mm_nt(g, st))
+            gp = (gf * sq_s[blk(b), c]).astype(BF16)
             gq_s[blk(b), c] = mm_nt(gp, qm_ref[h]).astype(BF16)
             p = mm_tn(q_s[blk(b), c], gp)
             total = p if total is None else total + p
-        send_part(h, total)
+        send_part((h // hh) * heads + lax.rem(h, hh), total)
 
     def finish_k(h):
         c = cols(h)
@@ -240,24 +260,127 @@
         for b in range(2):
             af = afters[b]
             cb = col_s[h, blk(b), :]
-            tot = cb[BLOCK - 1 : BLOCK]
             row = cum_s[pl.ds(h, 1), blk(b)]
-            weight = jnp.exp(jnp.where(iota1 >= iota0, row - wide(cb), -1e30))
-            qf, v, g = qf_s[blk(b), c], v_s[blk(b), c], g_s[blk(b), c]
-            probs = (mm_nt(kf_s[blk(b), c], qf) * weight).astype(BF16)
-            gv_s[blk(b), c] = (scale * (mm(probs, g) + mm(kd_s[blk(b), c], af))).astype(BF16)
-            gs = (mm_nt(v, g) * weight).astype(BF16)
-            gf = scale * (mm(gs, qf) + jnp.exp(tot - cb) * mm_nt(v, af))
-            gp = (gf * slope(prek_s[blk(b), c])).astype(BF16)
+            w0 = stack(
+                masked_exp(iota1 >= iota0, row[:, low] - cb[low]),
+                jnp.exp(row[:, high] - cb[low]),
+                1,
+            )
+            w1 = masked_exp(iota1 >= iota0, row[:, high] - cb[high])
+            qf, kf, v, g = qf_s[blk(b), c], kf_s[blk(b), c], v_s[blk(b), c], g_s[blk(b), c]
+            p0 = (mm_nt(kf[low], qf) * w0).astype(BF16)
+            p1 = (mm_nt(kf[high], qf[high]) * w1).astype(BF16)
+            intra = stack(mm(p0, g), mm(p1, g[high]), 0)
+            gv_s[blk(b), c] = (scale * (intra + mm(kd_s[blk(b), c], af))).astype(BF16)
+            g0 = (mm_nt(v[low], g) * w0).astype(BF16)
+            g1 = (mm_nt(v[high], g[high]) * w1).astype(BF16)
+            intra = stack(mm(g0, qf), mm(g1, qf[high]), 0)
+            gf = scale * (intra + ek_s[h, blk(b), :] * mm_nt(v, af))
+            gp = (gf * sk_s[blk(b), c]).astype(BF16)
             gk_s[blk(b), c] = mm_nt(gp, km_ref[h]).astype(BF16)
             p = mm_tn(k_s[blk(b), c], gp)
             total = p if total is None else total + p
-        send_part(heads + h, total)
+        send_part((h // hh) * heads + hh + lax.rem(h, hh), total)
+
+    size = own_s.shape[0] // (groups * n)
+
+    def piece(t, i):
+        return pl.ds(pl.multiple_of((t * n + i) * size, size), size)
+
+    def back(r):
+        return lax.rem(me + n - r, n)
+
+    def ctx_copy(t, r):
+        to = lax.rem(me + r, n)
+        return pltpu.make_async_remote_copy(
+            src_ref=own_s.at[piece(t, to)], dst_ref=cin_s.at[t, r - 1],
+            send_sem=c_send.at[t, r - 1], recv_sem=c_recv.at[t, r - 1],
+            device_id=(to, d), device_id_type=MESH,
+        )
+
+    def gather_copy(t, r, i):
+        return pltpu.make_async_remote_copy(
+            src_ref=res_s.at[d, piece(t, i)], dst_ref=res_s.at[d, piece(t, i)],
+            send_sem=ag_send.at[t, r - 1], recv_sem=ag_recv.at[t, r - 1],
+            device_id=(lax.rem(me + r, n), d), device_id_type=MESH,
+        )
+
+    across = lax.rem(d + 2, nd)
+    beside = d + 1 - 2 * lax.rem(d, 2)
+    diagonal = lax.rem(beside + 2, nd)
+
+    def y_copy(t, r, whose):
+        at = piece(t, back(r))
+        return pltpu.make_async_remote_copy(
+            src_ref=res_s.at[whose, at], dst_ref=res_s.at[whose, at],
+            send_sem=y_send.at[t, r], recv_sem=y_recv.at[t, r],
+            device_id=(me, across), device_id_type=MESH,
+        )
+
+    def core_copy(t, r, i, whose):
+        at = piece(t, back(r))
+        return pltpu.make_async_remote_copy(
+            src_ref=res_s.at[whose, at], dst_ref=res_s.at[whose, at],
+            send_sem=k_send.at[t, i, r], recv_sem=k_recv.at[t, i, r],
+            device_id=(me, beside), device_id_type=MESH,
+        )
+
+    def reduce_dp(t):
+        @pl.loop(0, 2 * hh)
+        def _(i):
+            m = t * 2 * hh + i
+            total = part_s[d, m]
+            for r in range(1, nd):
+                part_copy(m, r).wait_recv()
+                total = total + pin_s[r - 1, m]
+            own_s[pl.ds(pl.multiple_of(m * rows, rows), rows), :] = total
+
+        @pl.loop(1, n)
+        def _(r):
+            ctx_copy(t, r).start()
+
+    def reduce_ctx(t):
+        res_s[d, piece(t, me)] = own_s[piece(t, me)]
+
+        @pl.loop(1, n)
+        def _(r):
+            ctx_copy(t, r).wait_recv()
+            res_s[d, piece(t, me)] = res_s[d, piece(t, me)] + cin_s[t, r - 1]
+
+        @pl.loop(1, n)
+        def _(r):
+            gather_copy(t, r, me).start()
+
+        y_copy(t, 0, d).start()
+        core_copy(t, 0, 0, d).start()
+
+    def gather_ctx(t):
+        @pl.loop(1, n)
+        def _(r):
+            gather_copy(t, r, back(r)).wait_recv()
+            y_copy(t, r, d).start()
+            core_copy(t, r, 0, d).start()
+
+    def gather_y(t):
+        @pl.loop(0, n)
+        def _(r):
+            y_copy(t, r, across).wait_recv()
+            core_copy(t, r, 1, across).start()
+
+    def gather_core(t):
+        @pl.loop(0, n)
+        def _(r):
+            core_copy(t, r, 0, beside).wait_recv()
+            core_copy(t, r, 1, diagonal).wait_recv()
+
+    stages = (reduce_dp, reduce_ctx, gather_ctx, gather_y)
+    steps = heads + 2 * (nz - 1) + 2
+    ready = hh + 2 * (nz - 1) + 2
 
     def inside(h):
         return jnp.logical_and(h >= 0, h < heads)
 
-    @pl.loop(0, heads + 2 * (nz - 1) + 2)
+    @pl.loop(0, steps)
     def _(s):
         hf = s - 2 * z
         ha = s - 2 * (nz - 1 - z)
@@ -281,6 +404,10 @@
         @pl.when(inside(ha - 2))
         def _():
             finish_k(ha - 2)
+
+        if groups == 2:
+            for i, stage in enumerate(stages):
+                pl.when(s == ready + i)(functools.partial(stage, 0))
 
     stores = [
         pltpu.make_async_copy(src, dst, out_sem.at[i])
@@ -288,96 +415,10 @@
     ]
     for copy in stores:
         copy.start()
-
-    @pl.loop(0, 2 * heads)
-    def _(m):
-        total = part_s[d, m]
-        for r in range(1, nd):
-            part_copy(m, r).wait_recv()
-            total = total + pin_s[r - 1, m]
-        own_s[pl.ds(pl.multiple_of(m * rows, rows), rows), :] = total
-
-    size = own_s.shape[0] // n
-
-    def piece(i):
-        return pl.ds(pl.multiple_of(i * size, size), size)
-
-    def ctx_copy(r):
-        to = lax.rem(me + r, n)
-        return pltpu.make_async_remote_copy(
-            src_ref=own_s.at[piece(to)], dst_ref=cin_s.at[r - 1],
-            send_sem=c_send.at[r - 1], recv_sem=c_recv.at[r - 1],
-            device_id=(to, d), device_id_type=MESH,
-        )
-
-    @pl.loop(1, n)
-    def _(r):
-        ctx_copy(r).start()
-
-    res_s[d, piece(me)] = own_s[piece(me)]
-
-    @pl.loop(1, n)
-    def _(r):
-        ctx_copy(r).wait_recv()
-        res_s[d, piece(me)] = res_s[d, piece(me)] + cin_s[r - 1]
-
-    def gather_copy(r):
-        return pltpu.make_async_remote_copy(
-            src_ref=res_s.at[d, piece(me)], dst_ref=res_s.at[d, piece(me)],
-            send_sem=ag_send.at[r - 1], recv_sem=ag_recv.at[r - 1],
-            device_id=(lax.rem(me + r, n), d), device_id_type=MESH,
-        )
-
-    def gather_arrival(r):
-        at = piece(lax.rem(me + n - r, n))
-        return pltpu.make_async_remote_copy(
-            src_ref=res_s.at[d, at], dst_ref=res_s.at[d, at],
-            send_sem=ag_send.at[r - 1], recv_sem=ag_recv.at[r - 1],
-            device_id=(lax.rem(me + r, n), d), device_id_type=MESH,
-        )
-
-    across = lax.rem(d + 2, nd)
-    beside = d + 1 - 2 * lax.rem(d, 2)
-    diagonal = lax.rem(beside + 2, nd)
-
-    def y_copy(r, whose):
-        at = piece(lax.rem(me + n - r, n))
-        return pltpu.make_async_remote_copy(
-            src_ref=res_s.at[whose, at], dst_ref=res_s.at[whose, at],
-            send_sem=y_send.at[r], recv_sem=y_recv.at[r],
-            device_id=(me, across), device_id_type=MESH,
-        )
-
-    def core_copy(r, i, whose):
-        at = piece(lax.rem(me + n - r, n))
-        return pltpu.make_async_remote_copy(
-            src_ref=res_s.at[whose, at], dst_ref=res_s.at[whose, at],
-            send_sem=k_send.at[i, r], recv_sem=k_recv.at[i, r],
-            device_id=(me, beside), device_id_type=MESH,
-        )
-
-    @pl.loop(1, n)
-    def _(r):
-        gather_copy(r).start()
-
-    @pl.loop(0, n)
-    def _(r):
-        @pl.when(r > 0)
-        def _():
-            gather_arrival(r).wait_recv()
-
-        y_copy(r, d).start()
-        core_copy(r, 0, d).start()
-
-    @pl.loop(0, n)
-    def _(r):
-        y_copy(r, across).wait_recv()
-        core_copy(r, 1, across).start()
-
-    @pl.loop(0, n)
-    def _(r):
-        core_copy(r, 0, beside).wait_recv()
-        core_copy(r, 1, diagonal).wait_recv()
+    for stage in stages:
+        stage(groups - 1)
+    for t in range(groups):
+        gather_core(t)
 
     result = pltpu.make_async_copy(res_s, res_h, out_sem.at[4])
     result.start()
@@ -396,20 +437,43 @@
         for r in range(1, nd):
             part_copy(m, r).wait_send()
 
-    @pl.loop(1, n)
-    def _(r):
-        ctx_copy(r).wait_send()
-        gather_copy(r).wait_send()
-
-    @pl.loop(0, n)
-    def _(r):
-        y_copy(r, d).wait_send()
-        core_copy(r, 0, d).wait_send()
-        core_copy(r, 1, across).wait_send()
+    for t in range(groups):
+
+        @pl.loop(1, n)
+        def _(r):
+            ctx_copy(t, r).wait_send()
+            gather_copy(t, r, me).wait_send()
+
+        @pl.loop(0, n)
+        def _(r):
+            y_copy(t, r, d).wait_send()
+            core_copy(t, r, 0, d).wait_send()
+            core_copy(t, r, 1, across).wait_send()
 
     for copy in stores:
         copy.wait()
     result.wait()
+
+
+def place(nd, groups, hh, rows, a0, a1, a2, a3, maps, b0, b1, b2, b3, qm, km, sem, map_sem):
+    copies = [
+        pltpu.make_async_copy(src, dst, sem.at[i])
+        for i, (src, dst) in enumerate(((a0, b0), (a1, b1), (a2, b2), (a3, b3)))
+    ]
+    for i in range(nd):
+        for t in range(groups):
+            for w, dst in enumerate((qm, km)):
+                copies.append(
+                    pltpu.make_async_copy(
+                        maps.at[i, pl.ds((2 * t + w) * hh, hh)],
+                        dst.at[pl.ds(t * hh, hh), pl.ds(i * rows, rows)],
+                        map_sem.at[i, t, w],
+                    )
+                )
+    for copy in copies:
+        copy.start()
+    for copy in copies:
+        copy.wait()
 
 
 def solution(mesh):
@@ -421,6 +485,8 @@
         wide = heads * width
         rows = width // nd
         owned = 2 * heads * rows
+        groups = 2 if owned % (2 * 8 * n) == 0 else 1
+        hh = heads // groups
         any_spec = pl.BlockSpec(memory_space=pl.ANY)
         vmem_spec = pl.BlockSpec(memory_space=pltpu.VMEM)
         act = pltpu.VMEM((tokens, wide), BF16)
@@ -429,7 +495,7 @@
         mats2 = pltpu.VMEM((2, heads, width, width), F32)
         dma = pltpu.SemaphoreType.DMA
         outs = pl.pallas_call(
-            functools.partial(kernel, n, nd, heads, width, tokens),
+            functools.partial(kernel, n, nd, groups, heads, width, tokens),
             out_shape=[jax.ShapeDtypeStruct((tokens, wide), BF16)] * 4
             + [jax.ShapeDtypeStruct((nd, owned, width), F32)],
             in_specs=[any_spec, any_spec, any_spec, vmem_spec, any_spec, vmem_spec, vmem_spec],
@@ -440,6 +506,8 @@
             + [
                 pltpu.VMEM((heads, tokens), F32),
                 pltpu.VMEM((heads, tokens, width), F32),
+                pltpu.VMEM((heads, tokens, width), F32),
+                pltpu.VMEM((heads, tokens, width), F32),
                 pltpu.VMEM((heads, width), F32),
                 pltpu.VMEM((heads, width), F32),
             ]
@@ -449,7 +517,7 @@
                 pltpu.VMEM((nd, 2 * heads, rows, width), F32),
                 pltpu.VMEM((nd - 1, 2 * heads, rows, width), F32),
                 pltpu.VMEM((owned, width), F32),
-                pltpu.VMEM((n - 1, owned // n, width), F32),
+                pltpu.VMEM((groups, n - 1, owned // (groups * n), width), F32),
                 pltpu.VMEM((nd, owned, width), F32),
             ]
             + [
@@ -462,25 +530,33 @@
                 dma((2, heads)),
                 dma((nd - 1, 2 * heads)),
                 dma((nd - 1, 2 * heads)),
-                dma((n - 1,)),
-                dma((n - 1,)),
-                dma((n - 1,)),
-                dma((n - 1,)),
-                dma((n,)),
-                dma((n,)),
-                dma((2, n)),
-                dma((2, n)),
+                dma((groups, n - 1)),
+                dma((groups, n - 1)),
+                dma((groups, n - 1)),
+                dma((groups, n - 1)),
+                dma((groups, n)),
+                dma((groups, n)),
+                dma((groups, 2, n)),
+                dma((groups, 2, n)),
             ],
             compiler_params=pltpu.CompilerParams(
-                collective_id=0, has_side_effects=True, vmem_limit_bytes=48 * 1024 * 1024
+                collective_id=0, has_side_effects=True, vmem_limit_bytes=60 * 1024 * 1024
             ),
             cost_estimate=pl.CostEstimate(
                 flops=4_000_000_000, bytes_accessed=10_000_000, transcendentals=4_000_000
             ),
         )(query[0], key[0], value[0], log_decay[0], grad_out[0], query_map, key_map)
-        maps = outs[4].reshape(nd, 2, heads, rows, width).transpose(1, 2, 0, 3, 4)
-        maps = maps.reshape(2, heads, width, width)
-        return (outs[0][None], outs[1][None], outs[2][None], outs[3][None], maps[0], maps[1])
+        maps = outs[4].reshape(nd, 2 * heads, rows, width)
+        final = pl.pallas_call(
+            functools.partial(place, nd, groups, hh, rows),
+            out_shape=[jax.ShapeDtypeStruct((tokens, wide), BF16)] * 4
+            + [jax.ShapeDtypeStruct((heads, width, width), F32)] * 2,
+            in_specs=[any_spec] * 5,
+            out_specs=[any_spec] * 6,
+            scratch_shapes=[dma((4,)), dma((nd, groups, 2))],
+            compiler_params=pltpu.CompilerParams(vmem_limit_bytes=60 * 1024 * 1024),
+        )(*outs[:4], maps)
+        return tuple(a[None] for a in final[:4]) + tuple(final[4:])
 
     return jax.shard_map(
         local,

time: 74.2 us -> 229 us (3.09)
  Pallas kernels: 65 us -> 229 us
  local copies, waits for them, and re-layouts: 8.27 us -> 0 us
    pallas_call x1 -> x2, Pallas kernels: 65 us -> 229 us  [the longest x1 160 us: local(): pl.pallas_call(functools.partial(place, nd, groups, hh, rows), out_shape=...]
    unnamed x10 -> x0, local copies, waits for them, and re-layouts: 6.49 us -> none
where the time goes in v2:
time: 229 us
  Pallas kernels  229 us (100%)
    pallas_call x1, Pallas kernels, local(): pl.pallas_call(functools.partial(place, nd, groups, hh, rows), out_shape=...  160 us
    pallas_call x1, Pallas kernels, local(): pl.pallas_call(functools.partial(kernel, n, nd, groups, heads, width, tok...  68.6 us

profile of v2, /device:TPU:1, one launch (start us, length us, event | category | flops | bytes accessed | tf_op | source)
XLA Modules:
  0.0 229.3 jit_solution(15646058583194023122)
XLA Ops:
  0.6 68.6 %shard_map.118 = (bf16[512,1024]{1,0:T(8,128)(2,1)}, bf16[512,1024]{1,0:T(8,128)(2,1)}, bf16[512,1024]{1,0:T(8,128)(2,1)}, bf16[512,1024]{1,0:T(8,128)(2,1)}, f32[4,512,128]{2,1,0:T(8,128)}) custom-call(bf16[512,1024]{1,0:T(8,128)(2,1)} %bitcast.11, bf16[512,1024]{1,0:T(8,128)(2,1)} %bitcast.12, bf16[512,1024]{1,0:T(8,128)(2,1)} %bitcast.13, ...), custom_call_target="tpu_custom_call" | custom-call | flops 4000000000 | bytes 10000000 | tf_op jit(solution)/shard_map/pallas_call | solution.py:497
  69.2 160.1 %shard_map.119 = (bf16[512,1024]{1,0:T(8,128)(2,1)}, bf16[512,1024]{1,0:T(8,128)(2,1)}, bf16[512,1024]{1,0:T(8,128)(2,1)}, bf16[512,1024]{1,0:T(8,128)(2,1)}, f3...) custom-call(bf16[512,1024]{1,0:T(8,128)(2,1)} %get-tuple-element.17.a0, bf16[512,1024]{1,0:T(8,128)(2,1)} %get-tuple-element.18.a1, ...), custom_call_target="tpu_custom_call" | custom-call | tf_op jit(solution)/shard_map/pallas_call | solution.py:550

commit v3 on v2

--- a/solution.py
+++ b/solution.py
@@ -143,19 +143,21 @@
         C_s[h] = w[0] + d0 * w[1]
         c1_s[h] = w[1]
 
-    def chain_copy(way, h):
+    def chain_copy(way, p):
         to = z + 1 if way == 0 else z - 1
         to = jnp.clip(to, 0, nz - 1) * 2 + x
+        at = pl.ds(2 * p, 2)
         return pltpu.make_async_remote_copy(
-            src_ref=fout_s.at[way, h], dst_ref=fin_s.at[way, h],
-            send_sem=ch_send.at[way, h], recv_sem=ch_recv.at[way, h],
+            src_ref=fout_s.at[way, at], dst_ref=fin_s.at[way, at],
+            send_sem=ch_send.at[way, p], recv_sem=ch_recv.at[way, p],
             device_id=(to, d), device_id_type=MESH,
         )
 
-    def cross_copy(way, h):
+    def cross_copy(way, p):
+        at = pl.ds(2 * p, 2)
         return pltpu.make_async_remote_copy(
-            src_ref=xout_s.at[way, h], dst_ref=xin_s.at[way, h],
-            send_sem=x_send.at[way, h], recv_sem=x_recv.at[way, h],
+            src_ref=xout_s.at[way, at], dst_ref=xin_s.at[way, at],
+            send_sem=x_send.at[way, p], recv_sem=x_recv.at[way, p],
             device_id=(partner, d), device_id_type=MESH,
         )
 
@@ -168,46 +170,49 @@
     def has_out(way):
         return (z < nz - 1) if way == 0 else (z > 0)
 
-    def chain(way, h):
+    def chain(way, p):
         @pl.when(has_in(way))
         def _():
-            chain_copy(way, h).wait_recv()
-
-        own = mine_s[pl.ds(h, 1), :]
-        other = theirs_s[pl.ds(h, 1), :]
-        state = fin_s[way, h]
-        term = (U_s if way == 0 else C_s)[h]
+            chain_copy(way, p).wait_recv()
+
         first = is_first(way)
+        source = U_s if way == 0 else C_s
 
         @pl.when(has_out(way))
         def _():
-            carry = jnp.where(first, jnp.exp(other), 1.0)
-            fout_s[way, h] = jnp.exp(own + other) * state + carry * term
-            chain_copy(way, h).start()
-
-        keep = jnp.where(first, jnp.exp(own), 1.0)
-        xout_s[way, h] = keep * state + jnp.where(first, term, 0.0)
-        cross_copy(way, h).start()
+            for h in (2 * p, 2 * p + 1):
+                own = mine_s[pl.ds(h, 1), :]
+                other = theirs_s[pl.ds(h, 1), :]
+                carry = jnp.where(first, jnp.exp(other), 1.0)
+                fout_s[way, h] = jnp.exp(own + other) * fin_s[way, h] + carry * source[h]
+            chain_copy(way, p).start()
+
+        for h in (2 * p, 2 * p + 1):
+            keep = jnp.where(first, jnp.exp(mine_s[pl.ds(h, 1), :]), 1.0)
+            xout_s[way, h] = keep * fin_s[way, h] + jnp.where(first, source[h], 0.0)
+        cross_copy(way, p).start()
 
     def entering(way, h):
-        cross_copy(way, h).wait_recv()
         other = theirs_s[pl.ds(h, 1), :]
         keep = jnp.where(is_first(way), 1.0, jnp.exp(other))
         return keep * fin_s[way, h] + xin_s[way, h]
 
-    def part_copy(m, r):
+    def part_copy(i, r):
         to = lax.rem(d + r, nd)
+        at = pl.ds(2 * i, 2)
         return pltpu.make_async_remote_copy(
-            src_ref=part_s.at[to, m], dst_ref=pin_s.at[r - 1, m],
-            send_sem=p_send.at[r - 1, m], recv_sem=p_recv.at[r - 1, m],
+            src_ref=part_s.at[to, at], dst_ref=pin_s.at[r - 1, at],
+            send_sem=p_send.at[r - 1, i], recv_sem=p_recv.at[r - 1, i],
             device_id=(me, to), device_id_type=MESH,
         )
 
-    def send_part(m, part):
+    def keep_part(m, part):
         for i in range(nd):
             part_s[i, m] = part[i * rows : (i + 1) * rows]
+
+    def send_parts(i):
         for r in range(1, nd):
-            part_copy(m, r).start()
+            part_copy(i, r).start()
 
     half = BLOCK // 2
     iota0 = lax.broadcasted_iota(jnp.int32, (half, half), 0)
@@ -249,7 +254,7 @@
             gq_s[blk(b), c] = mm_nt(gp, qm_ref[h]).astype(BF16)
             p = mm_tn(q_s[blk(b), c], gp)
             total = p if total is None else total + p
-        send_part((h // hh) * heads + lax.rem(h, hh), total)
+        keep_part((h // hh) * heads + lax.rem(h, hh), total)
 
     def finish_k(h):
         c = cols(h)
@@ -280,7 +285,18 @@
             gk_s[blk(b), c] = mm_nt(gp, km_ref[h]).astype(BF16)
             p = mm_tn(k_s[blk(b), c], gp)
             total = p if total is None else total + p
-        send_part((h // hh) * heads + hh + lax.rem(h, hh), total)
+        keep_part((h // hh) * heads + hh + lax.rem(h, hh), total)
+
+    def first_passes(p):
+        first_pass(2 * p)
+        first_pass(2 * p + 1)
+
+    def finish(way, p):
+        cross_copy(way, p).wait_recv()
+        for h in (2 * p, 2 * p + 1):
+            (finish_q if way == 0 else finish_k)(h)
+        hp = hh // 2
+        send_parts((p // hp) * (heads // 2) + way * hp + lax.rem(p, hp))
 
     size = own_s.shape[0] // (groups * n)
 
@@ -326,14 +342,16 @@
         )
 
     def reduce_dp(t):
-        @pl.loop(0, 2 * hh)
-        def _(i):
-            m = t * 2 * hh + i
-            total = part_s[d, m]
+        @pl.loop(0, hh)
+        def _(j):
+            i = t * hh + j
+            at = pl.ds(2 * i, 2)
+            total = part_s[d, at]
             for r in range(1, nd):
-                part_copy(m, r).wait_recv()
-                total = total + pin_s[r - 1, m]
-            own_s[pl.ds(pl.multiple_of(m * rows, rows), rows), :] = total
+                part_copy(i, r).wait_recv()
+                total = total + pin_s[r - 1, at]
+            span = pl.ds(pl.multiple_of(2 * i * rows, 2 * rows), 2 * rows)
+            own_s[span, :] = total.reshape(2 * rows, width)
 
         @pl.loop(1, n)
         def _(r):
@@ -374,39 +392,40 @@
             core_copy(t, r, 1, diagonal).wait_recv()
 
     stages = (reduce_dp, reduce_ctx, gather_ctx, gather_y)
-    steps = heads + 2 * (nz - 1) + 2
-    ready = hh + 2 * (nz - 1) + 2
-
-    def inside(h):
-        return jnp.logical_and(h >= 0, h < heads)
+    pairs = heads // 2
+    steps = pairs + nz + 1
+    ready = hh // 2 + nz + 1
+
+    def inside(p):
+        return jnp.logical_and(p >= 0, p < pairs)
 
     @pl.loop(0, steps)
     def _(s):
-        hf = s - 2 * z
-        ha = s - 2 * (nz - 1 - z)
-
-        @pl.when(s < heads)
+        pf = s - 1 - z
+        pa = s - 1 - (nz - 1 - z)
+
+        @pl.when(inside(pf))
         def _():
-            first_pass(s)
-
-        @pl.when(inside(hf))
+            chain(0, pf)
+
+        @pl.when(inside(pa))
         def _():
-            chain(0, hf)
-
-        @pl.when(inside(ha))
+            chain(1, pa)
+
+        @pl.when(s < pairs)
         def _():
-            chain(1, ha)
-
-        @pl.when(inside(hf - 2))
+            first_passes(s)
+
+        @pl.when(inside(pf - 1))
         def _():
-            finish_q(hf - 2)
-
-        @pl.when(inside(ha - 2))
+            finish(0, pf - 1)
+
+        @pl.when(inside(pa - 1))
         def _():
-            finish_k(ha - 2)
+            finish(1, pa - 1)
 
         if groups == 2:
-            for i, stage in enumerate(stages):
+            for i, stage in enumerate(stages[:2]):
                 pl.when(s == ready + i)(functools.partial(stage, 0))
 
     stores = [
@@ -415,27 +434,35 @@
     ]
     for copy in stores:
         copy.start()
-    for stage in stages:
-        stage(groups - 1)
+    if groups == 2:
+        reduce_dp(1)
+        gather_ctx(0)
+        reduce_ctx(1)
+        gather_y(0)
+        gather_ctx(1)
+        gather_y(1)
+    else:
+        for stage in stages:
+            stage(0)
     for t in range(groups):
         gather_core(t)
 
     result = pltpu.make_async_copy(res_s, res_h, out_sem.at[4])
     result.start()
 
-    @pl.loop(0, heads)
-    def _(h):
+    @pl.loop(0, pairs)
+    def _(p):
         for way in range(2):
-            cross_copy(way, h).wait_send()
+            cross_copy(way, p).wait_send()
 
             @pl.when(has_out(way))
             def _():
-                chain_copy(way, h).wait_send()
-
-    @pl.loop(0, 2 * heads)
-    def _(m):
+                chain_copy(way, p).wait_send()
+
+    @pl.loop(0, heads)
+    def _(i):
         for r in range(1, nd):
-            part_copy(m, r).wait_send()
+            part_copy(i, r).wait_send()
 
     for t in range(groups):
 
@@ -455,24 +482,32 @@
     result.wait()
 
 
-def place(nd, groups, hh, rows, a0, a1, a2, a3, maps, b0, b1, b2, b3, qm, km, sem, map_sem):
-    copies = [
-        pltpu.make_async_copy(src, dst, sem.at[i])
-        for i, (src, dst) in enumerate(((a0, b0), (a1, b1), (a2, b2), (a3, b3)))
-    ]
+def place(nd, groups, hh, rows, a0, a1, a2, a3, maps, b0, b1, b2, b3, qm, km, held, mats, sem, map_sem):
+    pairs = ((a0, b0), (a1, b1), (a2, b2), (a3, b3))
+    loads = [pltpu.make_async_copy(maps, mats, sem.at[0, 4])]
+    loads += [pltpu.make_async_copy(src, held.at[i], sem.at[0, i]) for i, (src, _) in enumerate(pairs)]
+    for copy in loads:
+        copy.start()
+    stores = []
     for i in range(nd):
         for t in range(groups):
             for w, dst in enumerate((qm, km)):
-                copies.append(
+                stores.append(
                     pltpu.make_async_copy(
-                        maps.at[i, pl.ds((2 * t + w) * hh, hh)],
+                        mats.at[i, pl.ds((2 * t + w) * hh, hh)],
                         dst.at[pl.ds(t * hh, hh), pl.ds(i * rows, rows)],
                         map_sem.at[i, t, w],
                     )
                 )
-    for copy in copies:
+    loads[0].wait()
+    for copy in stores:
         copy.start()
-    for copy in copies:
+    for i, (_, dst) in enumerate(pairs):
+        loads[1 + i].wait()
+        copy = pltpu.make_async_copy(held.at[i], dst, sem.at[1, i])
+        copy.start()
+        stores.append(copy)
+    for copy in stores:
         copy.wait()
 
 
@@ -524,12 +559,12 @@
                 dma((4,)),
                 dma((5,)),
                 dma((2,)),
-                dma((2, heads)),
-                dma((2, heads)),
-                dma((2, heads)),
-                dma((2, heads)),
-                dma((nd - 1, 2 * heads)),
-                dma((nd - 1, 2 * heads)),
+                dma((2, heads // 2)),
+                dma((2, heads // 2)),
+                dma((2, heads // 2)),
+                dma((2, heads // 2)),
+                dma((nd - 1, heads)),
+                dma((nd - 1, heads)),
                 dma((groups, n - 1)),
                 dma((groups, n - 1)),
                 dma((groups, n - 1)),
@@ -553,8 +588,13 @@
             + [jax.ShapeDtypeStruct((heads, width, width), F32)] * 2,
             in_specs=[any_spec] * 5,
             out_specs=[any_spec] * 6,
-            scratch_shapes=[dma((4,)), dma((nd, groups, 2))],
-            compiler_params=pltpu.CompilerParams(vmem_limit_bytes=60 * 1024 * 1024),
+            scratch_shapes=[
+                pltpu.VMEM((4, tokens, wide), BF16),
+                pltpu.VMEM((nd, 2 * heads, rows, width), F32),
+                dma((2, 5)),
+                dma((nd, groups, 2)),
+            ],
+            compiler_params=pltpu.CompilerParams(vmem_limit_bytes=48 * 1024 * 1024),
         )(*outs[:4], maps)
         return tuple(a[None] for a in final[:4]) + tuple(final[4:])
 

time: 229 us -> 76.4 us (0.33)
  Pallas kernels: 229 us -> 69.3 us
  local copies, waits for them, and re-layouts: 0 us -> 6.11 us
    pallas_call x1, Pallas kernels: 160 us -> 2.92 us  [local(): pl.pallas_call(functools.partial(place, nd, groups, hh, rows), out_shape=...]
    unnamed x0 -> x10, local copies, waits for them, and re-layouts: none -> 6.11 us
where the time goes in v3:
time: 76.4 us; the launch traced here: 76.1 us
  Pallas kernels  69.3 us (91%)
  local copies, waits for them, and re-layouts  6.11 us (8%)
    pallas_call x1, Pallas kernels, local(): pl.pallas_call(functools.partial(kernel, n, nd, groups, heads, width, tok...  66.4 us
    unnamed x10, local copies, waits for them, and re-layouts  6.11 us
    pallas_call x1, Pallas kernels, local(): pl.pallas_call(functools.partial(place, nd, groups, hh, rows), out_shape=...  2.92 us

profile of v3, /device:TPU:1, one launch (start us, length us, event | category | flops | bytes accessed | tf_op | source)
XLA Modules:
  0.0 76.1 jit_solution(17014389288180109078)
XLA Ops:
  0.6 66.4 %shard_map.118 = (bf16[512,1024]{1,0:T(8,128)(2,1)}, bf16[512,1024]{1,0:T(8,128)(2,1)}, bf16[512,1024]{1,0:T(8,128)(2,1)}, bf16[512,1024]{1,0:T(8,128)(2,1)}, f32[4,512,128]{2,1,0:T(8,128)}) custom-call(bf16[512,1024]{1,0:T(8,128)(2,1)} %bitcast.11, bf16[512,1024]{1,0:T(8,128)(2,1)} %bitcast.12, bf16[512,1024]{1,0:T(8,128)(2,1)} %bitcast.13, ...), custom_call_target="tpu_custom_call" | custom-call | flops 4000000000 | bytes 10000000 | tf_op jit(solution)/shard_map/pallas_call | solution.py:532
  67.0 0.0 copy-start
  67.1 1.2 %copy-done = bf16[512,1024]{1,0:T(8,128)(2,1)S(1)} copy-done((bf16[512,1024]{1,0:T(8,128)(2,1)S(1)}, bf16[512,1024]{1,0:T(8,128)(2,1)}, u32[]{:S(2)}) %copy-start) | copy-done | bytes 1048600
  68.3 0.0 copy-start.1
  68.3 1.2 %copy-done.1 = bf16[512,1024]{1,0:T(8,128)(2,1)S(1)} copy-done((bf16[512,1024]{1,0:T(8,128)(2,1)S(1)}, bf16[512,1024]{1,0:T(8,128)(2,1)}, u32[]{:S(2)}) %copy-start.1) | copy-done | bytes 1048600
  69.5 0.0 copy-start.2
  69.5 1.2 %copy-done.2 = bf16[512,1024]{1,0:T(8,128)(2,1)S(1)} copy-done((bf16[512,1024]{1,0:T(8,128)(2,1)S(1)}, bf16[512,1024]{1,0:T(8,128)(2,1)}, u32[]{:S(2)}) %copy-start.2) | copy-done | bytes 1048600
  70.7 0.0 copy-start.3
  70.7 1.2 %copy-done.3 = bf16[512,1024]{1,0:T(8,128)(2,1)S(1)} copy-done((bf16[512,1024]{1,0:T(8,128)(2,1)S(1)}, bf16[512,1024]{1,0:T(8,128)(2,1)}, u32[]{:S(2)}) %copy-start.3) | copy-done | bytes 1048600
  72.0 0.0 copy-start.4
  72.0 1.2 %copy-done.4 = f32[4,512,128]{2,1,0:T(8,128)S(1)} copy-done((f32[4,512,128]{2,1,0:T(8,128)S(1)}, f32[4,512,128]{2,1,0:T(8,128)}, u32[]{:S(2)}) %copy-start.4) | copy-done | bytes 1048600
  73.2 2.9 %shard_map.119 = (bf16[512,1024]{1,0:T(8,128)(2,1)}, bf16[512,1024]{1,0:T(8,128)(2,1)}, bf16[512,1024]{1,0:T(8,128)(2,1)}, bf16[512,1024]{1,0:T(8,128)(2,1)}, f3...) custom-call(bf16[512,1024]{1,0:T(8,128)(2,1)S(1)} %copy-done, bf16[512,1024]{1,0:T(8,128)(2,1)S(1)} %copy-done.1, ...), custom_call_target="tpu_custom_call" | custom-call | tf_op jit(solution)/shard_map/pallas_call | solution.py:585
Async XLA Ops:
  67.0 1.2 %copy-start = (bf16[512,1024]{1,0:T(8,128)(2,1)S(1)}, bf16[512,1024]{1,0:T(8,128)(2,1)}, u32[]{:S(2)}) copy-start(bf16[512,1024]{1,0:T(8,128)(2,1)} %get-tuple-element.17.a0) | copy-start | bytes 3145732
  68.3 1.2 %copy-start.1 = (bf16[512,1024]{1,0:T(8,128)(2,1)S(1)}, bf16[512,1024]{1,0:T(8,128)(2,1)}, u32[]{:S(2)}) copy-start(bf16[512,1024]{1,0:T(8,128)(2,1)} %get-tuple-element.18.a1) | copy-start | bytes 3145732
  69.5 1.2 %copy-start.2 = (bf16[512,1024]{1,0:T(8,128)(2,1)S(1)}, bf16[512,1024]{1,0:T(8,128)(2,1)}, u32[]{:S(2)}) copy-start(bf16[512,1024]{1,0:T(8,128)(2,1)} %get-tuple-element.19.a2) | copy-start | bytes 3145732
  70.7 1.2 %copy-start.3 = (bf16[512,1024]{1,0:T(8,128)(2,1)S(1)}, bf16[512,1024]{1,0:T(8,128)(2,1)}, u32[]{:S(2)}) copy-start(bf16[512,1024]{1,0:T(8,128)(2,1)} %get-tuple-element.20.a3) | copy-start | bytes 3145732
  72.0 1.2 %copy-start.4 = (f32[4,512,128]{2,1,0:T(8,128)S(1)}, f32[4,512,128]{2,1,0:T(8,128)}, u32[]{:S(2)}) copy-start(f32[4,512,128]{2,1,0:T(8,128)} %get-tuple-element.21) | copy-start | bytes 3145732

commit v4 on v3

--- a/solution.py
+++ b/solution.py
@@ -99,7 +99,6 @@
     decay_copy.start()
     for copy in loads:
         copy.wait()
-    decay_copy.wait()
 
     def cols(h):
         return pl.ds(pl.multiple_of(h * width, width), width)
@@ -403,6 +402,10 @@
     def _(s):
         pf = s - 1 - z
         pa = s - 1 - (nz - 1 - z)
+
+        @pl.when(s == 1)
+        def _():
+            decay_copy.wait()
 
         @pl.when(inside(pf))
         def _():
@@ -594,7 +597,7 @@
                 dma((2, 5)),
                 dma((nd, groups, 2)),
             ],
-            compiler_params=pltpu.CompilerParams(vmem_limit_bytes=48 * 1024 * 1024),
+            compiler_params=pltpu.CompilerParams(vmem_limit_bytes=60 * 1024 * 1024),
         )(*outs[:4], maps)
         return tuple(a[None] for a in final[:4]) + tuple(final[4:])
 

time: 76.4 us -> 70.4 us (0.921)
  local copies, waits for them, and re-layouts: 6.11 us -> 0 us
    unnamed x10 -> x0, local copies, waits for them, and re-layouts: 6.11 us -> none
    pallas_call x1, Pallas kernels: 2.92 us -> 4.52 us  [local(): pl.pallas_call(functools.partial(place, nd, groups, hh, rows), out_shape=...]
    pallas_call x1, Pallas kernels: 66.4 us -> 65.1 us  [local(): pl.pallas_call(functools.partial(kernel, n, nd, groups, heads, width, tok...]
where the time goes in v4:
time: 70.4 us; the launch traced here: 70.3 us
  Pallas kernels  69.7 us (99%)
    pallas_call x1, Pallas kernels, local(): pl.pallas_call(functools.partial(kernel, n, nd, groups, heads, width, tok...  65.1 us
    pallas_call x1, Pallas kernels, local(): pl.pallas_call(functools.partial(place, nd, groups, hh, rows), out_shape=...  4.52 us

profile of v4, /device:TPU:1, one launch (start us, length us, event | category | flops | bytes accessed | tf_op | source)
XLA Modules:
  0.0 70.3 jit_solution(13030541142438640831)
XLA Ops:
  0.6 65.1 %shard_map.118 = (bf16[512,1024]{1,0:T(8,128)(2,1)}, bf16[512,1024]{1,0:T(8,128)(2,1)}, bf16[512,1024]{1,0:T(8,128)(2,1)}, bf16[512,1024]{1,0:T(8,128)(2,1)}, f32[4,512,128]{2,1,0:T(8,128)}) custom-call(bf16[512,1024]{1,0:T(8,128)(2,1)} %bitcast.11, bf16[512,1024]{1,0:T(8,128)(2,1)} %bitcast.12, bf16[512,1024]{1,0:T(8,128)(2,1)} %bitcast.13, ...), custom_call_target="tpu_custom_call" | custom-call | flops 4000000000 | bytes 10000000 | tf_op jit(solution)/shard_map/pallas_call | solution.py:535
  65.8 4.5 %shard_map.119 = (bf16[512,1024]{1,0:T(8,128)(2,1)}, bf16[512,1024]{1,0:T(8,128)(2,1)}, bf16[512,1024]{1,0:T(8,128)(2,1)}, bf16[512,1024]{1,0:T(8,128)(2,1)}, f3...) custom-call(bf16[512,1024]{1,0:T(8,128)(2,1)} %get-tuple-element.17.a0, bf16[512,1024]{1,0:T(8,128)(2,1)} %get-tuple-element.18.a1, ...), custom_call_target="tpu_custom_call" | custom-call | tf_op jit(solution)/shard_map/pallas_call | solution.py:588

commit v5 on v4

--- a/solution.py
+++ b/solution.py
@@ -419,17 +419,20 @@
         def _():
             first_passes(s)
 
-        @pl.when(inside(pf - 1))
-        def _():
-            finish(0, pf - 1)
-
-        @pl.when(inside(pa - 1))
-        def _():
-            finish(1, pa - 1)
-
         if groups == 2:
             for i, stage in enumerate(stages[:2]):
                 pl.when(s == ready + i)(functools.partial(stage, 0))
+
+        @pl.when(inside(pf - 1))
+        def _():
+            finish(0, pf - 1)
+
+        @pl.when(inside(pa - 1))
+        def _():
+            finish(1, pa - 1)
+
+        if groups == 2:
+            pl.when(s == ready + 1)(functools.partial(gather_ctx, 0))
 
     stores = [
         pltpu.make_async_copy(src, dst, out_sem.at[i])
@@ -439,9 +442,8 @@
         copy.start()
     if groups == 2:
         reduce_dp(1)
-        gather_ctx(0)
+        gather_y(0)
         reduce_ctx(1)
-        gather_y(0)
         gather_ctx(1)
         gather_y(1)
     else:

time: 70.4 us -> 71.5 us (1.016)
  Pallas kernels: 69.7 us -> 70.7 us
    pallas_call x1, Pallas kernels: 65.1 us -> 66.2 us  [local(): pl.pallas_call(functools.partial(kernel, n, nd, groups, heads, width, tok...]
where the time goes in v5:
time: 71.5 us; the launch traced here: 71.3 us
  Pallas kernels  70.7 us (99%)
    pallas_call x1, Pallas kernels, local(): pl.pallas_call(functools.partial(kernel, n, nd, groups, heads, width, tok...  66.2 us
    pallas_call x1, Pallas kernels, local(): pl.pallas_call(functools.partial(place, nd, groups, hh, rows), out_shape=...  4.52 us

profile of v5, /device:TPU:1, one launch (start us, length us, event | category | flops | bytes accessed | tf_op | source)
XLA Modules:
  0.0 71.3 jit_solution(854802427003160970)
XLA Ops:
  0.6 66.2 %shard_map.118 = (bf16[512,1024]{1,0:T(8,128)(2,1)}, bf16[512,1024]{1,0:T(8,128)(2,1)}, bf16[512,1024]{1,0:T(8,128)(2,1)}, bf16[512,1024]{1,0:T(8,128)(2,1)}, f32[4,512,128]{2,1,0:T(8,128)}) custom-call(bf16[512,1024]{1,0:T(8,128)(2,1)} %bitcast.11, bf16[512,1024]{1,0:T(8,128)(2,1)} %bitcast.12, bf16[512,1024]{1,0:T(8,128)(2,1)} %bitcast.13, ...), custom_call_target="tpu_custom_call" | custom-call | flops 4000000000 | bytes 10000000 | tf_op jit(solution)/shard_map/pallas_call | solution.py:537
  66.8 4.5 %shard_map.119 = (bf16[512,1024]{1,0:T(8,128)(2,1)}, bf16[512,1024]{1,0:T(8,128)(2,1)}, bf16[512,1024]{1,0:T(8,128)(2,1)}, bf16[512,1024]{1,0:T(8,128)(2,1)}, f3...) custom-call(bf16[512,1024]{1,0:T(8,128)(2,1)} %get-tuple-element.17.a0, bf16[512,1024]{1,0:T(8,128)(2,1)} %get-tuple-element.18.a1, ...), custom_call_target="tpu_custom_call" | custom-call | tf_op jit(solution)/shard_map/pallas_call | solution.py:590
